TPU v7x, 32 devices: a whole 2x2x4 slice. The times are simulated.
32 devices in a mesh: depth: 4 (over y, x), tile: 8 (over z, core).
Axes of the slice: x: 2, y: 2, z: 4, core: 2. Of those that a mesh axis runs over, the one named last changes fastest.
Arguments:
- volume: float32 [64, 512, 2048], P('depth', 'tile'), may hold values from -6 to 6
- entry_depth: int32 [512, 2048], P('tile'), may hold values from 0 to 31
- light_dir: float32 [3], replicated, may hold values from 0.2 to 1
- transfer: float32 [4, 3], replicated, may hold values from -6 to 6
Outputs:
- frame_rgba: float32 [4, 512, 2048], P(None, 'tile', 'depth')
All inputs are finite; a program needn't handle non-finite values.
Results may differ from a plain program's by a relative error of at most 0.0003.
Values sent between devices are 32-bit elements; how exact they have to be, the bound alone decides.
A program may use at most 128 MiB of HBM per device.

v0:
```python
import functools

import jax
import jax.numpy as jnp
from jax import lax
from jax.experimental import pallas as pl
from jax.experimental.pallas import tpu as pltpu
from jax.sharding import PartitionSpec as P

LANES = 128
PAD = 8
BLOCK = 32
LOG2E = 1.4426950408889634


def kernel(groups, tiles, depth_total, volume, entry_hbm, light_hbm, transfer_hbm, out, entry, light, transfer, vol, top_out, bottom_out, top_in,
           bottom_in, sent, got, passing, small_sem, load_sem, front_sem, back_sem, row_sem, piece_send, piece_recv, pass_send, pass_recv):
    slab, rows, columns = volume.shape
    strips = columns // LANES
    own = strips // groups
    me, tile = lax.axis_index("depth"), lax.axis_index("tile")
    body = pl.ds(PAD, rows)

    def load(strip):
        return pltpu.make_async_copy(
            volume.at[:, :, pl.ds(pl.multiple_of(strip * LANES, LANES), LANES)],
            vol.at[pl.ds(1, slab), strip + 1, body, :],
            load_sem.at[strip],
        )

    def front(strip):
        return pltpu.make_async_remote_copy(
            src_ref=volume.at[slab - 1, :, pl.ds(pl.multiple_of(strip * LANES, LANES), LANES)],
            dst_ref=vol.at[0, strip + 1, body, :],
            send_sem=front_sem.at[0, strip],
            recv_sem=front_sem.at[1, strip],
            device_id={"depth": lax.rem(me + 1, groups)},
            device_id_type=pl.DeviceIdType.MESH,
        )

    def back(strip):
        return pltpu.make_async_remote_copy(
            src_ref=volume.at[0, :, pl.ds(pl.multiple_of(strip * LANES, LANES), LANES)],
            dst_ref=vol.at[slab + 1, strip + 1, body, :],
            send_sem=back_sem.at[0, strip],
            recv_sem=back_sem.at[1, strip],
            device_id={"depth": lax.rem(me + groups - 1, groups)},
            device_id_type=pl.DeviceIdType.MESH,
        )

    def row_copy(src, dst, way, target):
        return pltpu.make_async_remote_copy(
            src_ref=src,
            dst_ref=dst,
            send_sem=row_sem.at[0, way],
            recv_sem=row_sem.at[1, way],
            device_id={"tile": target},
            device_id_type=pl.DeviceIdType.MESH,
        )

    def piece(strip, target, source, k):
        return pltpu.make_async_remote_copy(
            src_ref=sent.at[strip],
            dst_ref=got.at[source, k],
            send_sem=piece_send.at[strip],
            recv_sem=piece_recv.at[source, k],
            device_id={"depth": target},
            device_id_type=pl.DeviceIdType.MESH,
        )

    relays = own // 2 if groups == 4 else 0
    middle = jnp.logical_and(me > 0, me < groups - 1)

    def pass_in(strip, k):
        return pltpu.make_async_remote_copy(
            src_ref=sent.at[strip],
            dst_ref=passing.at[k],
            send_sem=piece_send.at[strip],
            recv_sem=pass_recv.at[k],
            device_id={"depth": lax.rem(me + 2, groups)},
            device_id_type=pl.DeviceIdType.MESH,
        )

    def pass_on(k):
        target = jnp.where(me == 0, 1, 2)
        source = 3 - target
        return pltpu.make_async_remote_copy(
            src_ref=passing.at[k],
            dst_ref=got.at[source, k],
            send_sem=pass_send.at[k],
            recv_sem=piece_recv.at[source, k],
            device_id={"depth": target},
            device_id_type=pl.DeviceIdType.MESH,
        )

    def strip_at(step, device):
        k = step // groups
        target = lax.rem(device + 1 + lax.rem(step, groups), groups)
        return target * own + k, target, k

    up, down = lax.rem(tile + tiles - 1, tiles), lax.rem(tile + 1, tiles)
    to_lower = row_copy(bottom_out, top_in, 0, down)
    to_upper = row_copy(top_out, bottom_in, 1, up)

    small = [
        pltpu.make_async_copy(src, dst, small_sem.at[i])
        for i, (src, dst) in enumerate(((entry_hbm, entry), (light_hbm, light), (transfer_hbm, transfer)))
    ]

    @pl.loop(0, strips)
    def _(strip):
        load(strip).start()

    for copy in small:
        copy.start()

    barrier = pltpu.get_barrier_semaphore()
    for hop in range(1, groups):
        pl.semaphore_signal(barrier, inc=1, device_id={"depth": lax.rem(me + hop, groups)},
                            device_id_type=pl.DeviceIdType.MESH)
    for target in (up, down):
        pl.semaphore_signal(barrier, inc=1, device_id={"tile": target}, device_id_type=pl.DeviceIdType.MESH)
    pl.semaphore_wait(barrier, groups + 1)

    @pl.loop(0, strips)
    def _(step):
        @pl.when(me < groups - 1)
        def _():
            front(strip_at(step, me + 1)[0]).start()

        @pl.when(me > 0)
        def _():
            back(strip_at(step, me - 1 + groups)[0]).start()

    zeros = jnp.zeros((rows, LANES), jnp.float32)

    @pl.when(me == 0)
    def _():
        @pl.loop(0, strips)
        def _(strip):
            vol[0, strip + 1, body, :] = zeros

    @pl.when(me == groups - 1)
    def _():
        @pl.loop(0, strips)
        def _(strip):
            vol[slab + 1, strip + 1, body, :] = zeros

    @pl.loop(0, slab)
    def _(layer):
        vol[layer + 1, 0, body, :] = zeros
        vol[layer + 1, strips + 1, body, :] = zeros

    @pl.loop(0, strips)
    def _(strip):
        load(strip).wait()
        for layer in range(slab):
            top_out[strip, pl.ds(layer, 1), :] = vol[layer + 1, strip + 1, pl.ds(PAD, 1), :]
            bottom_out[strip, pl.ds(layer, 1), :] = vol[layer + 1, strip + 1, pl.ds(PAD + rows - 1, 1), :]

    @pl.when(tile < tiles - 1)
    def _():
        to_lower.start()

    @pl.when(tile > 0)
    def _():
        to_upper.start()

    @pl.when(tile == 0)
    def _():
        top_in[...] = jnp.zeros_like(top_in)

    @pl.when(tile == tiles - 1)
    def _():
        bottom_in[...] = jnp.zeros_like(bottom_in)

    @pl.when(tile > 0)
    def _():
        to_lower.wait_recv()

    @pl.when(tile < tiles - 1)
    def _():
        to_upper.wait_recv()

    @pl.loop(0, strips)
    def _(strip):
        for layer in range(slab):
            vol[layer + 1, strip + 1, pl.ds(PAD - 1, 1), :] = top_in[strip, pl.ds(layer, 1), :]
            vol[layer + 1, strip + 1, pl.ds(PAD + rows, 1), :] = bottom_in[strip, pl.ds(layer, 1), :]

    for copy in small:
        copy.wait()

    shape = (BLOCK, LANES)
    light_sq = light[0] * light[0] + light[1] * light[1] + light[2] * light[2]
    light_scale = 0.175 * lax.rsqrt(jnp.full(shape, light_sq, jnp.float32))
    light_z, light_x, light_y = (light[i] * light_scale for i in range(3))
    tone = [[0.5 * transfer[k, j] for j in range(3)] for k in range(3)]
    thick = [-LOG2E * transfer[3, j] for j in range(3)]
    lane = lax.broadcasted_iota(jnp.int32, shape, 1)
    first, last = lane == 0, lane == LANES - 1
    peak = 4.0 / depth_total

    @pl.loop(0, strips)
    def _(step):
        strip, target, k = strip_at(step, me)
        at = strip + 1

        @pl.when(me > 0)
        def _():
            front(strip).wait_recv()

        @pl.when(me < groups - 1)
        def _():
            back(strip).wait_recv()

        for low in range(0, rows, BLOCK):
            here = pl.ds(PAD + low, BLOCK)
            entered = entry[pl.ds(low, BLOCK), pl.ds(pl.multiple_of(strip * LANES, LANES), LANES)] - me * slab
            before, value = vol[0, at, here, :], vol[1, at, here, :]
            clear = jnp.ones(shape, jnp.float32)
            total = jnp.zeros(shape, jnp.float32)
            base = jnp.zeros(shape, jnp.float32)
            sums = [jnp.zeros(shape, jnp.float32)] * 3
            for layer in range(slab):
                after = vol[layer + 2, at, here, :]
                grad_z = after - before
                grad_x = vol[layer + 1, at, pl.ds(PAD + low + 1, BLOCK), :] - vol[
                    layer + 1, at, pl.ds(PAD + low - 1, BLOCK), :]
                right = jnp.where(first, vol[layer + 1, at + 1, here, :], value)
                left = jnp.where(last, vol[layer + 1, at - 1, here, :], value)
                grad_y = pltpu.roll(right, LANES - 1, 1) - pltpu.roll(left, 1, 1)
                square = 0.25 * (grad_z * grad_z + grad_x * grad_x + grad_y * grad_y) + 1.0
                inverse = lax.rsqrt(square)
                norm = square * inverse
                facing = jnp.abs(light_z * grad_z + light_x * grad_x + light_y * grad_y)
                half_shade = 0.15 + facing * inverse
                spread = 1.0 + jnp.exp2(jnp.minimum(thick[0] * value + thick[1] * norm + thick[2], 126.0))
                guess = pl.reciprocal(spread, approx=True)
                opacity = peak * (guess * (2.0 - spread * guess))
                opacity = jnp.where(entered <= layer, opacity, 0.0)
                weight = clear * opacity
                clear = clear - weight
                total = total + weight
                lit = weight * half_shade
                base = base + lit
                for c in range(3):
                    sums[c] = sums[c] + lit * jnp.tanh(tone[c][0] * value + tone[c][1] * norm + tone[c][2])
                before, value = value, after
            for c in range(3):
                sent[strip, c, pl.ds(low, BLOCK), :] = base + sums[c]
            sent[strip, 3, pl.ds(low, BLOCK), :] = total

        relayed = jnp.logical_and(jnp.logical_and(middle, target == 3 - me), k < relays)

        @pl.when(jnp.logical_and(target != me, jnp.logical_not(relayed)))
        def _():
            piece(strip, target, me, k).start()

        if relays:
            @pl.when(relayed)
            def _():
                pass_in(strip, k).start()

            @pl.when(jnp.logical_and(jnp.logical_not(middle), jnp.logical_and(lax.rem(step, groups) == 0, k >= own - relays)))
            def _():
                pass_in(strip, k - (own - relays)).wait_recv()
                pass_on(k - (own - relays)).start()

        @pl.when(target == me)
        def _():
            got[me, k] = sent[strip]

    for k in range(own):
        for hop in range(1, groups):
            source = lax.rem(me + hop, groups)
            piece(source * own + k, source, source, k).wait_recv()
        for low in range(0, rows, BLOCK):
            here = pl.ds(low, BLOCK)
            clear = jnp.ones(shape, jnp.float32)
            sums = [jnp.zeros(shape, jnp.float32)] * 4
            for source in range(groups):
                alpha = got[source, k, 3, here, :]
                for c in range(3):
                    sums[c] = sums[c] + clear * got[source, k, c, here, :]
                sums[3] = sums[3] + clear * alpha
                clear = clear - clear * alpha
            for c in range(4):
                out[c, here, pl.ds(k * LANES, LANES)] = sums[c]

    @pl.loop(0, strips)
    def _(step):
        strip, target, k = strip_at(step, me)

        @pl.when(me < groups - 1)
        def _():
            front(strip).wait_send()

        @pl.when(me > 0)
        def _():
            back(strip).wait_send()

        @pl.when(target != me)
        def _():
            piece(strip, target, me, k).wait_send()

    if relays:
        @pl.when(jnp.logical_not(middle))
        def _():
            for k in range(relays):
                pass_on(k).wait_send()

    @pl.when(tile < tiles - 1)
    def _():
        to_lower.wait_send()

    @pl.when(tile > 0)
    def _():
        to_upper.wait_send()


def local(volume, entry_depth, light_dir, transfer):
    slab, rows, columns = volume.shape
    groups, tiles = lax.axis_size("depth"), lax.axis_size("tile")
    strips = columns // LANES
    own = strips // groups
    edge = pltpu.VMEM((strips, slab, LANES), jnp.float32)
    return pl.pallas_call(
        functools.partial(kernel, groups, tiles, float(slab * groups)),
        out_shape=jax.ShapeDtypeStruct((4, rows, columns // groups), jnp.float32),
        in_specs=[pl.BlockSpec(memory_space=pl.ANY)] * 4,
        out_specs=pl.BlockSpec(memory_space=pltpu.VMEM),
        scratch_shapes=[
            pltpu.VMEM((rows, columns), jnp.int32),
            pltpu.SMEM((3,), jnp.float32),
            pltpu.SMEM((4, 3), jnp.float32),
            pltpu.VMEM((slab + 2, strips + 2, rows + 2 * PAD, LANES), jnp.float32),
            edge,
            edge,
            edge,
            edge,
            pltpu.VMEM((strips, 4, rows, LANES), jnp.float32),
            pltpu.VMEM((groups, own, 4, rows, LANES), jnp.float32),
            pltpu.VMEM((max(own // 2, 1), 4, rows, LANES), jnp.float32),
            pltpu.SemaphoreType.DMA((3,)),
            pltpu.SemaphoreType.DMA((strips,)),
            pltpu.SemaphoreType.DMA((2, strips)),
            pltpu.SemaphoreType.DMA((2, strips)),
            pltpu.SemaphoreType.DMA((2, 2)),
            pltpu.SemaphoreType.DMA((strips,)),
            pltpu.SemaphoreType.DMA((groups, own)),
            pltpu.SemaphoreType.DMA((max(own // 2, 1),)),
            pltpu.SemaphoreType.DMA((max(own // 2, 1),)),
        ],
        compiler_params=pltpu.CompilerParams(
            collective_id=0, has_side_effects=True, vmem_limit_bytes=60 * 1024 * 1024
        ),
        cost_estimate=pl.CostEstimate(
            flops=60 * slab * rows * columns, bytes_accessed=4 * slab * rows * columns, transcendentals=6 * slab * rows * columns
        ),
    )(volume, entry_depth, light_dir, transfer)


def solution(mesh):
    placed = (P("depth", "tile", None), P("tile", None), P(), P())
    return jax.shard_map(
        local, mesh=mesh, in_specs=placed, out_specs=P(None, "tile", "depth"), check_vma=False
    )
```

profile of v0, /device:TPU:0, one launch (start us, length us, event | category | flops | bytes accessed | tf_op | source)
XLA Modules:
  0.0 49.2 jit_solution(11160345450657204871)
XLA Ops:
  0.0 47.4 %shard_map.46 = f32[4,64,512]{2,1,0:T(8,128)} custom-call(f32[16,64,2048]{2,1,0:T(8,128)} %volume.1, s32[64,2048]{1,0:T(8,128)} %entry_hbm.1, f32[3]{0:T(128)} %light_hbm.1, f32[4,3]{1,0:T(4,128)} %transfer_hbm.1), custom_call_target="tpu_custom_call" | custom-call | flops 125829120 | bytes 8388608 | tf_op jit(solution)/shard_map/pallas_call | solution.py:328
  47.4 1.9 %copy.6 = f32[4,64,512]{2,1,0:T(8,128)} copy(f32[4,64,512]{2,1,0:T(8,128)} %shard_map.46) | data formatting | bytes 1048576
where the time goes:
time: 49.4 us; the launch traced here: 49.2 us
  Pallas kernels  47.4 us (96%)
  local copies, waits for them, and re-layouts  1.87 us (4%)
    pallas_call x1, Pallas kernels, local(): pl.pallas_call(functools.partial(kernel, groups, tiles, float(slab * grou...  47.4 us
    unnamed x1, local copies, waits for them, and re-layouts  1.87 us

commit v1 on v0

--- a/solution.py
+++ b/solution.py
@@ -94,8 +94,10 @@
         )
 
     def strip_at(step, device):
-        k = step // groups
-        target = lax.rem(device + 1 + lax.rem(step, groups), groups)
+        others = groups - 1
+        away = step < own * others
+        k = jnp.where(away, step // others, step - own * others)
+        target = lax.rem(device + jnp.where(away, 1 + lax.rem(step, others), 0), groups)
         return target * own + k, target, k
 
     up, down = lax.rem(tile + tiles - 1, tiles), lax.rem(tile + 1, tiles)
@@ -262,7 +264,7 @@
             def _():
                 pass_in(strip, k).start()
 
-            @pl.when(jnp.logical_and(jnp.logical_not(middle), jnp.logical_and(lax.rem(step, groups) == 0, k >= own - relays)))
+            @pl.when(jnp.logical_and(jnp.logical_not(middle), jnp.logical_and(target == lax.rem(me + 1, groups), k >= own - relays)))
             def _():
                 pass_in(strip, k - (own - relays)).wait_recv()
                 pass_on(k - (own - relays)).start()

time: 49.4 us -> 49.5 us (level)
  no operation moved by 1% of the time
where the time goes in v1:
time: 49.5 us; the launch traced here: 49.3 us
  Pallas kernels  47.4 us (96%)
  local copies, waits for them, and re-layouts  1.87 us (4%)
    pallas_call x1, Pallas kernels, local(): pl.pallas_call(functools.partial(kernel, groups, tiles, float(slab * grou...  47.4 us
    unnamed x1, local copies, waits for them, and re-layouts  1.87 us

profile of v1, /device:TPU:0, one launch (start us, length us, event | category | flops | bytes accessed | tf_op | source)
XLA Modules:
  0.0 49.3 jit_solution(13494084877961232880)
XLA Ops:
  0.0 47.4 %shard_map.46 = f32[4,64,512]{2,1,0:T(8,128)} custom-call(f32[16,64,2048]{2,1,0:T(8,128)} %volume.1, s32[64,2048]{1,0:T(8,128)} %entry_hbm.1, f32[3]{0:T(128)} %light_hbm.1, f32[4,3]{1,0:T(4,128)} %transfer_hbm.1), custom_call_target="tpu_custom_call" | custom-call | flops 125829120 | bytes 8388608 | tf_op jit(solution)/shard_map/pallas_call | solution.py:330
  47.5 1.9 %copy.6 = f32[4,64,512]{2,1,0:T(8,128)} copy(f32[4,64,512]{2,1,0:T(8,128)} %shard_map.46) | data formatting | bytes 1048576

commit v2 on v1

--- a/solution.py
+++ b/solution.py
@@ -1,4 +1,5 @@
 import functools
+import math
 
 import jax
 import jax.numpy as jnp
@@ -9,7 +10,7 @@
 
 LANES = 128
 PAD = 8
-BLOCK = 32
+BLOCK = 16
 LOG2E = 1.4426950408889634
 
 
@@ -195,13 +196,14 @@
 
     shape = (BLOCK, LANES)
     light_sq = light[0] * light[0] + light[1] * light[1] + light[2] * light[2]
-    light_scale = 0.175 * lax.rsqrt(jnp.full(shape, light_sq, jnp.float32))
+    light_scale = 0.35 * lax.rsqrt(jnp.full(shape, light_sq, jnp.float32))
     light_z, light_x, light_y = (light[i] * light_scale for i in range(3))
-    tone = [[0.5 * transfer[k, j] for j in range(3)] for k in range(3)]
-    thick = [-LOG2E * transfer[3, j] for j in range(3)]
+    halves = (0.5, 0.25, 0.5)
+    tone = [[halves[j] * transfer[k, j] for j in range(3)] for k in range(3)]
+    peak = 4.0 / depth_total
+    thick = [-LOG2E * transfer[3, 0], -0.5 * LOG2E * transfer[3, 1], -LOG2E * transfer[3, 2] - math.log2(peak)]
     lane = lax.broadcasted_iota(jnp.int32, shape, 1)
     first, last = lane == 0, lane == LANES - 1
-    peak = 4.0 / depth_total
 
     @pl.loop(0, strips)
     def _(step):
@@ -232,14 +234,14 @@
                 right = jnp.where(first, vol[layer + 1, at + 1, here, :], value)
                 left = jnp.where(last, vol[layer + 1, at - 1, here, :], value)
                 grad_y = pltpu.roll(right, LANES - 1, 1) - pltpu.roll(left, 1, 1)
-                square = 0.25 * (grad_z * grad_z + grad_x * grad_x + grad_y * grad_y) + 1.0
+                square = (grad_z * grad_z + grad_x * grad_x) + (grad_y * grad_y + 4.0)
                 inverse = lax.rsqrt(square)
                 norm = square * inverse
                 facing = jnp.abs(light_z * grad_z + light_x * grad_x + light_y * grad_y)
                 half_shade = 0.15 + facing * inverse
-                spread = 1.0 + jnp.exp2(jnp.minimum(thick[0] * value + thick[1] * norm + thick[2], 126.0))
+                spread = 1.0 / peak + jnp.exp2(jnp.minimum(thick[0] * value + thick[1] * norm + thick[2], 126.0))
                 guess = pl.reciprocal(spread, approx=True)
-                opacity = peak * (guess * (2.0 - spread * guess))
+                opacity = guess * (2.0 - spread * guess)
                 opacity = jnp.where(entered <= layer, opacity, 0.0)
                 weight = clear * opacity
                 clear = clear - weight

time: 49.5 us -> 49.5 us (level)
  no operation moved by 1% of the time
where the time goes in v2:
time: 49.5 us; the launch traced here: 49.3 us
  Pallas kernels  47.5 us (96%)
  local copies, waits for them, and re-layouts  1.87 us (4%)
    pallas_call x1, Pallas kernels, local(): pl.pallas_call(functools.partial(kernel, groups, tiles, float(slab * grou...  47.5 us
    unnamed x1, local copies, waits for them, and re-layouts  1.87 us

profile of v2, /device:TPU:0, one launch (start us, length us, event | category | flops | bytes accessed | tf_op | source)
XLA Modules:
  0.0 49.3 jit_solution(14601260735129132904)
XLA Ops:
  0.0 47.5 %shard_map.46 = f32[4,64,512]{2,1,0:T(8,128)} custom-call(f32[16,64,2048]{2,1,0:T(8,128)} %volume.1, s32[64,2048]{1,0:T(8,128)} %entry_hbm.1, f32[3]{0:T(128)} %light_hbm.1, f32[4,3]{1,0:T(4,128)} %transfer_hbm.1), custom_call_target="tpu_custom_call" | custom-call | flops 125829120 | bytes 8388608 | tf_op jit(solution)/shard_map/pallas_call | solution.py:332
  47.5 1.9 %copy.6 = f32[4,64,512]{2,1,0:T(8,128)} copy(f32[4,64,512]{2,1,0:T(8,128)} %shard_map.46) | data formatting | bytes 1048576

commit v3 on v2

--- a/solution.py
+++ b/solution.py
@@ -14,8 +14,8 @@
 LOG2E = 1.4426950408889634
 
 
-def kernel(groups, tiles, depth_total, volume, entry_hbm, light_hbm, transfer_hbm, out, entry, light, transfer, vol, top_out, bottom_out, top_in,
-           bottom_in, sent, got, passing, small_sem, load_sem, front_sem, back_sem, row_sem, piece_send, piece_recv, pass_send, pass_recv):
+def kernel(groups, tiles, depth_total, volume, entry_hbm, light_hbm, transfer_hbm, got, entry, light, transfer, vol, top_out, bottom_out, top_in,
+           bottom_in, sent, passing, small_sem, load_sem, front_sem, back_sem, row_sem, piece_send, piece_recv, pass_send, pass_recv, own_sem):
     slab, rows, columns = volume.shape
     strips = columns // LANES
     own = strips // groups
@@ -62,11 +62,16 @@
     def piece(strip, target, source, k):
         return pltpu.make_async_remote_copy(
             src_ref=sent.at[strip],
-            dst_ref=got.at[source, k],
+            dst_ref=got.at[source, :, :, pl.ds(pl.multiple_of(k * LANES, LANES), LANES)],
             send_sem=piece_send.at[strip],
             recv_sem=piece_recv.at[source, k],
             device_id={"depth": target},
             device_id_type=pl.DeviceIdType.MESH,
+        )
+
+    def own_copy(strip, k):
+        return pltpu.make_async_copy(
+            sent.at[strip], got.at[me, :, :, pl.ds(pl.multiple_of(k * LANES, LANES), LANES)], own_sem.at[k]
         )
 
     relays = own // 2 if groups == 4 else 0
@@ -87,7 +92,7 @@
         source = 3 - target
         return pltpu.make_async_remote_copy(
             src_ref=passing.at[k],
-            dst_ref=got.at[source, k],
+            dst_ref=got.at[source, :, :, pl.ds(pl.multiple_of(k * LANES, LANES), LANES)],
             send_sem=pass_send.at[k],
             recv_sem=piece_recv.at[source, k],
             device_id={"depth": target},
@@ -273,24 +278,13 @@
 
         @pl.when(target == me)
         def _():
-            got[me, k] = sent[strip]
+            own_copy(strip, k).start()
 
     for k in range(own):
+        own_copy(me * own + k, k).wait()
         for hop in range(1, groups):
             source = lax.rem(me + hop, groups)
             piece(source * own + k, source, source, k).wait_recv()
-        for low in range(0, rows, BLOCK):
-            here = pl.ds(low, BLOCK)
-            clear = jnp.ones(shape, jnp.float32)
-            sums = [jnp.zeros(shape, jnp.float32)] * 4
-            for source in range(groups):
-                alpha = got[source, k, 3, here, :]
-                for c in range(3):
-                    sums[c] = sums[c] + clear * got[source, k, c, here, :]
-                sums[3] = sums[3] + clear * alpha
-                clear = clear - clear * alpha
-            for c in range(4):
-                out[c, here, pl.ds(k * LANES, LANES)] = sums[c]
 
     @pl.loop(0, strips)
     def _(step):
@@ -329,11 +323,11 @@
     strips = columns // LANES
     own = strips // groups
     edge = pltpu.VMEM((strips, slab, LANES), jnp.float32)
-    return pl.pallas_call(
+    got = pl.pallas_call(
         functools.partial(kernel, groups, tiles, float(slab * groups)),
-        out_shape=jax.ShapeDtypeStruct((4, rows, columns // groups), jnp.float32),
+        out_shape=jax.ShapeDtypeStruct((groups, 4, rows, columns // groups), jnp.float32),
         in_specs=[pl.BlockSpec(memory_space=pl.ANY)] * 4,
-        out_specs=pl.BlockSpec(memory_space=pltpu.VMEM),
+        out_specs=pl.BlockSpec(memory_space=pl.ANY),
         scratch_shapes=[
             pltpu.VMEM((rows, columns), jnp.int32),
             pltpu.SMEM((3,), jnp.float32),
@@ -344,7 +338,6 @@
             edge,
             edge,
             pltpu.VMEM((strips, 4, rows, LANES), jnp.float32),
-            pltpu.VMEM((groups, own, 4, rows, LANES), jnp.float32),
             pltpu.VMEM((max(own // 2, 1), 4, rows, LANES), jnp.float32),
             pltpu.SemaphoreType.DMA((3,)),
             pltpu.SemaphoreType.DMA((strips,)),
@@ -355,6 +348,7 @@
             pltpu.SemaphoreType.DMA((groups, own)),
             pltpu.SemaphoreType.DMA((max(own // 2, 1),)),
             pltpu.SemaphoreType.DMA((max(own // 2, 1),)),
+            pltpu.SemaphoreType.DMA((own,)),
         ],
         compiler_params=pltpu.CompilerParams(
             collective_id=0, has_side_effects=True, vmem_limit_bytes=60 * 1024 * 1024
@@ -363,6 +357,11 @@
             flops=60 * slab * rows * columns, bytes_accessed=4 * slab * rows * columns, transcendentals=6 * slab * rows * columns
         ),
     )(volume, entry_depth, light_dir, transfer)
+    frame, clear = got[0], 1.0 - got[0, 3]
+    for source in range(1, groups):
+        frame = frame + clear * got[source]
+        clear = clear * (1.0 - got[source, 3])
+    return frame
 
 
 def solution(mesh):

time: 49.5 us -> 51.5 us (1.040)
  other arithmetic: 0 us -> 4.58 us
  local copies, waits for them, and re-layouts: 1.87 us -> 0 us
  Pallas kernels: 47.5 us -> 46.7 us
    add x0 -> x1, other arithmetic: none -> 2.6 us  [local(): frame = frame + clear * got[source]]
    unnamed x1 -> x0, local copies, waits for them, and re-layouts: 1.87 us -> none
    mul x0 -> x1, other arithmetic: none -> 1.06 us  [local(): clear = clear * (1.0 - got[source, 3])]
    sub x0 -> x1, other arithmetic: none -> 0.92 us  [local(): frame, clear = (got[0], 1.0 - got[0, 3])]
    pallas_call x1, Pallas kernels: 47.5 us -> 46.7 us  [local(): pl.pallas_call(functools.partial(kernel, groups, tiles, float(slab * grou...]
where the time goes in v3:
time: 51.5 us; the launch traced here: 51.3 us
  Pallas kernels  46.7 us (91%)
  other arithmetic  4.58 us (9%)
    pallas_call x1, Pallas kernels, local(): pl.pallas_call(functools.partial(kernel, groups, tiles, float(slab * grou...  46.7 us
    add x1, other arithmetic, local(): frame = frame + clear * got[source]  2.6 us
    mul x1, other arithmetic, local(): clear = clear * (1.0 - got[source, 3])  1.06 us

profile of v3, /device:TPU:0, one launch (start us, length us, event | category | flops | bytes accessed | tf_op | source)
XLA Modules:
  0.0 51.3 jit_solution(10008341208588030233)
XLA Ops:
  0.0 46.7 %shard_map.46 = f32[4,4,64,512]{3,2,1,0:T(8,128)} custom-call(f32[16,64,2048]{2,1,0:T(8,128)} %volume.1, s32[64,2048]{1,0:T(8,128)} %entry_hbm.1, f32[3]{0:T(128)} %light_hbm.1, f32[4,3]{1,0:T(4,128)} %transfer_hbm.1), custom_call_target="tpu_custom_call" | custom-call | flops 125829120 | bytes 8388608 | tf_op jit(solution)/shard_map/pallas_call | solution.py:326
  46.7 0.9 %subtract_bitcast_fusion = f32[64,512]{1,0:T(8,128)S(1)} fusion(f32[4,4,64,512]{3,2,1,0:T(8,128)} %shard_map.46), kind=kLoop, calls=%fused_computation.8 | loop fusion | flops 32768 | bytes 262144 | tf_op jit(solution)/shard_map/sub | solution.py:360
  47.6 1.1 %bitcast_multiply_fusion.3 = (f32[64,512]{1,0:T(8,128)S(1)}, f32[64,512]{1,0:T(8,128)S(1)}) fusion(f32[4,4,64,512]{3,2,1,0:T(8,128)} %shard_map.46), kind=kLoop, calls=%fused_computation.6 | loop fusion | flops 163840 | bytes 655360 | tf_op jit(solution)/shard_map/mul | solution.py:363
  48.7 2.6 %fusion = f32[4,64,512]{2,1,0:T(8,128)} fusion(f32[4,4,64,512]{3,2,1,0:T(8,128)} %shard_map.46, f32[64,512]{1,0:T(8,128)S(1)} %get-tuple-element.5, f32[64,512]{1,0:T(8,128)S(1)} %get-tuple-element.6, f32[64,512]{1,0:T(8,128)S(1)} %subtract_bitcast_fusion), kind=kLoop, calls=%fused_computation.1 | loop fusion | flops 786432 | bytes 3014656 | tf_op jit(solution)/shard_map/add | solution.py:362

commit v4 on v2

--- a/solution.py
+++ b/solution.py
@@ -15,7 +15,7 @@
 
 
 def kernel(groups, tiles, depth_total, volume, entry_hbm, light_hbm, transfer_hbm, out, entry, light, transfer, vol, top_out, bottom_out, top_in,
-           bottom_in, sent, got, passing, small_sem, load_sem, front_sem, back_sem, row_sem, piece_send, piece_recv, pass_send, pass_recv):
+           bottom_in, sent, got, passing, detour, small_sem, load_sem, front_sem, back_sem, row_sem, piece_send, piece_recv, pass_send, pass_recv, hop_sem):
     slab, rows, columns = volume.shape
     strips = columns // LANES
     own = strips // groups
@@ -69,7 +69,7 @@
             device_id_type=pl.DeviceIdType.MESH,
         )
 
-    relays = own // 2 if groups == 4 else 0
+    relays, detours = 0, strips // 2 if groups == 4 else 0
     middle = jnp.logical_and(me > 0, me < groups - 1)
 
     def pass_in(strip, k):
@@ -92,6 +92,43 @@
             recv_sem=piece_recv.at[source, k],
             device_id={"depth": target},
             device_id_type=pl.DeviceIdType.MESH,
+        )
+
+    across, mate = lax.rem(me + 2, groups), me + 1 - 2 * lax.rem(me, 2)
+    outer = jnp.logical_not(middle)
+
+    def detour_in(step):
+        strip = strip_at(step, groups - 1 - me)[0]
+        slot = step - (strips - detours)
+        return pltpu.make_async_remote_copy(
+            src_ref=volume.at[jnp.where(me == 1, slab - 1, 0), :, pl.ds(pl.multiple_of(strip * LANES, LANES), LANES)],
+            dst_ref=detour.at[slot],
+            send_sem=hop_sem.at[0, slot],
+            recv_sem=hop_sem.at[1, slot],
+            device_id={"depth": across},
+            device_id_type=pl.DeviceIdType.MESH,
+        )
+
+    def detour_on(step, layer, sem):
+        strip = strip_at(step, mate)[0]
+        slot = step - (strips - detours)
+        return pltpu.make_async_remote_copy(
+            src_ref=detour.at[slot],
+            dst_ref=vol.at[layer, strip + 1, body, :],
+            send_sem=hop_sem.at[2, slot],
+            recv_sem=sem.at[1, strip],
+            device_id={"depth": mate},
+            device_id_type=pl.DeviceIdType.MESH,
+        )
+
+    def halo_ways(step):
+        ahead, behind = me < groups - 1, me > 0
+        if not detours:
+            return ahead, behind
+        early = step < strips - detours
+        return (
+            jnp.logical_and(ahead, jnp.logical_or(early, me != 1)),
+            jnp.logical_and(behind, jnp.logical_or(early, me != 2)),
         )
 
     def strip_at(step, device):
@@ -127,13 +164,20 @@
 
     @pl.loop(0, strips)
     def _(step):
-        @pl.when(me < groups - 1)
+        ahead, behind = halo_ways(step)
+
+        @pl.when(ahead)
         def _():
             front(strip_at(step, me + 1)[0]).start()
 
-        @pl.when(me > 0)
+        @pl.when(behind)
         def _():
             back(strip_at(step, me - 1 + groups)[0]).start()
+
+        if detours:
+            @pl.when(jnp.logical_and(middle, step >= strips - detours))
+            def _():
+                detour_in(step).start()
 
     zeros = jnp.zeros((rows, LANES), jnp.float32)
 
@@ -193,6 +237,21 @@
 
     for copy in small:
         copy.wait()
+
+    if detours:
+        @pl.when(outer)
+        def _():
+            @pl.loop(strips - detours, strips)
+            def _(step):
+                detour_in(step).wait_recv()
+
+                @pl.when(me == 0)
+                def _():
+                    detour_on(step, slab + 1, back_sem).start()
+
+                @pl.when(me != 0)
+                def _():
+                    detour_on(step, 0, front_sem).start()
 
     shape = (BLOCK, LANES)
     light_sq = light[0] * light[0] + light[1] * light[1] + light[2] * light[2]
@@ -296,13 +355,24 @@
     def _(step):
         strip, target, k = strip_at(step, me)
 
-        @pl.when(me < groups - 1)
-        def _():
-            front(strip).wait_send()
-
-        @pl.when(me > 0)
-        def _():
-            back(strip).wait_send()
+        ahead, behind = halo_ways(step)
+
+        @pl.when(ahead)
+        def _():
+            front(strip_at(step, me + 1)[0]).wait_send()
+
+        @pl.when(behind)
+        def _():
+            back(strip_at(step, me - 1 + groups)[0]).wait_send()
+
+        if detours:
+            @pl.when(jnp.logical_and(middle, step >= strips - detours))
+            def _():
+                detour_in(step).wait_send()
+
+            @pl.when(jnp.logical_and(outer, step >= strips - detours))
+            def _():
+                detour_on(step, 0, front_sem).wait_send()
 
         @pl.when(target != me)
         def _():
@@ -346,6 +416,7 @@
             pltpu.VMEM((strips, 4, rows, LANES), jnp.float32),
             pltpu.VMEM((groups, own, 4, rows, LANES), jnp.float32),
             pltpu.VMEM((max(own // 2, 1), 4, rows, LANES), jnp.float32),
+            pltpu.VMEM((strips // 2, rows, LANES), jnp.float32),
             pltpu.SemaphoreType.DMA((3,)),
             pltpu.SemaphoreType.DMA((strips,)),
             pltpu.SemaphoreType.DMA((2, strips)),
@@ -355,6 +426,7 @@
             pltpu.SemaphoreType.DMA((groups, own)),
             pltpu.SemaphoreType.DMA((max(own // 2, 1),)),
             pltpu.SemaphoreType.DMA((max(own // 2, 1),)),
+            pltpu.SemaphoreType.DMA((3, strips // 2)),
         ],
         compiler_params=pltpu.CompilerParams(
             collective_id=0, has_side_effects=True, vmem_limit_bytes=60 * 1024 * 1024

time: 49.5 us -> 49.9 us (level)
  no operation moved by 1% of the time
where the time goes in v4:
time: 49.9 us; the launch traced here: 49.7 us
  Pallas kernels  47.8 us (96%)
  local copies, waits for them, and re-layouts  1.87 us (4%)
    pallas_call x1, Pallas kernels, local(): pl.pallas_call(functools.partial(kernel, groups, tiles, float(slab * grou...  47.8 us
    unnamed x1, local copies, waits for them, and re-layouts  1.87 us

profile of v4, /device:TPU:0, one launch (start us, length us, event | category | flops | bytes accessed | tf_op | source)
XLA Modules:
  0.0 49.7 jit_solution(15113247547502104370)
XLA Ops:
  0.0 47.8 %shard_map.46 = f32[4,64,512]{2,1,0:T(8,128)} custom-call(f32[16,64,2048]{2,1,0:T(8,128)} %volume.1, s32[64,2048]{1,0:T(8,128)} %entry_hbm.1, f32[3]{0:T(128)} %light_hbm.1, f32[4,3]{1,0:T(4,128)} %transfer_hbm.1), custom_call_target="tpu_custom_call" | custom-call | flops 125829120 | bytes 8388608 | tf_op jit(solution)/shard_map/pallas_call | solution.py:402
  47.8 1.9 %copy.6 = f32[4,64,512]{2,1,0:T(8,128)} copy(f32[4,64,512]{2,1,0:T(8,128)} %shard_map.46) | data formatting | bytes 1048576

commit v5 on v2

--- a/solution.py
+++ b/solution.py
@@ -95,10 +95,8 @@
         )
 
     def strip_at(step, device):
-        others = groups - 1
-        away = step < own * others
-        k = jnp.where(away, step // others, step - own * others)
-        target = lax.rem(device + jnp.where(away, 1 + lax.rem(step, others), 0), groups)
+        k = step // groups
+        target = lax.rem(device + 1 + lax.rem(step, groups), groups)
         return target * own + k, target, k
 
     up, down = lax.rem(tile + tiles - 1, tiles), lax.rem(tile + 1, tiles)
@@ -266,7 +264,7 @@
             def _():
                 pass_in(strip, k).start()
 
-            @pl.when(jnp.logical_and(jnp.logical_not(middle), jnp.logical_and(target == lax.rem(me + 1, groups), k >= own - relays)))
+            @pl.when(jnp.logical_and(jnp.logical_not(middle), jnp.logical_and(lax.rem(step, groups) == 0, k >= own - relays)))
             def _():
                 pass_in(strip, k - (own - relays)).wait_recv()
                 pass_on(k - (own - relays)).start()

time: 49.5 us -> 49.4 us (level)
  no operation moved by 1% of the time
where the time goes in v5:
time: 49.4 us; the launch traced here: 49.3 us
  Pallas kernels  47.4 us (96%)
  local copies, waits for them, and re-layouts  1.87 us (4%)
    pallas_call x1, Pallas kernels, local(): pl.pallas_call(functools.partial(kernel, groups, tiles, float(slab * grou...  47.4 us
    unnamed x1, local copies, waits for them, and re-layouts  1.87 us

profile of v5, /device:TPU:0, one launch (start us, length us, event | category | flops | bytes accessed | tf_op | source)
XLA Modules:
  0.0 49.3 jit_solution(6255630897127966706)
XLA Ops:
  0.0 47.4 %shard_map.46 = f32[4,64,512]{2,1,0:T(8,128)} custom-call(f32[16,64,2048]{2,1,0:T(8,128)} %volume.1, s32[64,2048]{1,0:T(8,128)} %entry_hbm.1, f32[3]{0:T(128)} %light_hbm.1, f32[4,3]{1,0:T(4,128)} %transfer_hbm.1), custom_call_target="tpu_custom_call" | custom-call | flops 125829120 | bytes 8388608 | tf_op jit(solution)/shard_map/pallas_call | solution.py:330
  47.4 1.9 %copy.6 = f32[4,64,512]{2,1,0:T(8,128)} copy(f32[4,64,512]{2,1,0:T(8,128)} %shard_map.46) | data formatting | bytes 1048576
